TPU v7x, 32 devices: a whole 2x2x4 slice. The times are simulated.
32 devices in a mesh: dp: 8 (over z, x), tm: 4 (over y, core).
Axes of the slice: x: 2, y: 2, z: 4, core: 2. Of those that a mesh axis runs over, the one named last changes fastest.
Arguments:
- clip_input: bfloat16 [8, 8, 256, 384], P('dp', 'tm'), may hold values from -32 to 32
- norm_gain: float32 [384], replicated, may hold values from 0.1 to 1.9
- qkv_weight: bfloat16 [384, 1152], replicated, may hold values from -2 to 2
- out_weight: bfloat16 [384, 384], replicated, may hold values from -0.3125 to 0.3125
- time_weight: bfloat16 [3, 384, 768], P(None, 'dp'), may hold values from -0.1875 to 0.1875
- upsample_cotangent: bfloat16 [8, 8, 256, 768], P('dp', 'tm'), may hold values from -6 to 6
Outputs:
- input_grad: bfloat16 [8, 8, 256, 384], P('dp', 'tm')
- qkv_grad: float32 [384, 1152], P('dp', 'tm')
All inputs are finite; a program needn't handle non-finite values.
Results may differ from a plain program's by a relative error of at most 0.024.
Values may be sent and summed in bfloat16 or wider, within the bound.
A program may use at most 64 MiB of HBM per device.

v0:
```python
import functools
import math

import jax
import jax.numpy as jnp
from jax import lax
from jax.experimental import pallas as pl
from jax.experimental.pallas import tpu as pltpu
from jax.sharding import PartitionSpec as P


def passed_along(block, axis, distance):
    devices = range(lax.axis_size(axis))
    route = [(i - distance, i) for i in devices if i - distance in devices]
    return lax.ppermute(block, axis, route)


def rms_scaled(features, norm_gain):
    squares = jnp.mean(features * features, axis=-1, keepdims=True)
    return features * lax.rsqrt(squares + 1e-06) * norm_gain


def block_tail(qkv_rows, features, out_weight):
    width = features.shape[-1]
    queries = qkv_rows[..., :width]
    keys = qkv_rows[..., width : 2 * width]
    values = qkv_rows[..., 2 * width :]
    scores = jnp.einsum(
        "fqc,fkc->fqk", queries, keys, preferred_element_type=jnp.float32
    ) / math.sqrt(width)
    weights = jax.nn.softmax(scores, axis=-1).astype(jnp.bfloat16)
    mixed = jnp.einsum("fqk,fkc->fqc", weights, values, preferred_element_type=jnp.float32).astype(
        jnp.bfloat16
    )
    branch = jnp.einsum("fqc,cd->fqd", mixed, out_weight, preferred_element_type=jnp.float32)
    return (features + branch).astype(jnp.bfloat16)


def attention_grads(clip_rows, norm_gain, qkv_weight, out_weight, upstream):
    features = clip_rows.astype(jnp.float32)
    normed, pre_back = jax.vjp(lambda value: rms_scaled(value, norm_gain), features)
    normed_bf = normed.astype(jnp.bfloat16)
    qkv_rows = jnp.einsum(
        "fhc,cd->fhd", normed_bf, qkv_weight, preferred_element_type=jnp.float32
    ).astype(jnp.bfloat16)
    block_out, tail_back = jax.vjp(
        lambda first, second: block_tail(first, second, out_weight), qkv_rows, features
    )
    qkv_cot, feature_cot = tail_back(upstream)
    normed_cot = jnp.einsum("fhd,cd->fhc", qkv_cot, qkv_weight, preferred_element_type=jnp.float32)
    direct = pre_back(normed_cot)[0]
    input_grad = (feature_cot + direct).astype(jnp.bfloat16)
    return (input_grad, normed_bf, qkv_cot)


def on_device_by_collectives(clip_input, norm_gain, qkv_weight, out_weight, time_weight, upsample_cotangent):
    rows = clip_input[0]
    cotangent = upsample_cotangent[0]
    frames = cotangent.shape[0]
    width = rows.shape[-1]
    incoming = passed_along(cotangent, "tm", -1)
    padded = jnp.concatenate([cotangent, incoming], 0)
    piece = lax.all_gather(time_weight, "dp", axis=1, tiled=True)
    result = jnp.einsum(
        "fhd,cd->fhc", padded[2 : 2 + frames], piece[0], preferred_element_type=jnp.float32
    )
    result = result + jnp.einsum(
        "fhd,cd->fhc", padded[1 : 1 + frames], piece[1], preferred_element_type=jnp.float32
    )
    upstream = (
        result
        + jnp.einsum("fhd,cd->fhc", padded[0:frames], piece[2], preferred_element_type=jnp.float32)
    ).astype(jnp.bfloat16)
    input_grad, normed_bf, qkv_cot = attention_grads(
        rows, norm_gain, qkv_weight, out_weight, upstream
    )
    flat_normed = normed_bf.reshape(-1, width)
    flat_cot = qkv_cot.reshape(-1, 3 * width)
    shares = lax.psum_scatter(
        jnp.einsum("rc,rd->cd", flat_normed, flat_cot, preferred_element_type=jnp.float32).astype(
            jnp.bfloat16
        ),
        "dp",
        scatter_dimension=0,
        tiled=True,
    )
    qkv_grad = lax.psum_scatter(shares, "tm", scatter_dimension=1, tiled=True).astype(jnp.float32)
    return (input_grad[None], qkv_grad)


LANES = 128
VMEM_GRANT = 64 * 1024 * 1024 - 64 * 1024
MESH = pl.DeviceIdType.MESH
F32 = jnp.float32
BF16 = jnp.bfloat16
PLAIN = ((1,), (0,))
RIGHT_T = ((1,), (1,))
LEFT_T = ((0,), (0,))
CHUNKS = ((2, 1), (0, 2))


def matmul(a, b, contract):
    return lax.dot_general(a, b, (contract, ((), ())), preferred_element_type=F32)


def fused_kernel(
    nz,
    clip_hbm,
    gain_hbm,
    qkv_w_hbm,
    out_w_hbm,
    taps_hbm,
    cot_hbm,
    grad_in_hbm,
    grad_w_hbm,
    clip,
    gain,
    qkv_w,
    out_w,
    taps,
    cot,
    normed,
    normed_t,
    qkv,
    probs,
    weights_t,
    total,
    upstream,
    mixed_cot,
    qkv_cot,
    grad_in,
    grad_w,
    grad,
    pair_in,
    kept,
    x_out,
    x_in,
    z_out,
    z_in,
    slab,
    slab_in,
    local_sem,
    cot_send,
    cot_recv,
    z_send,
    line_recv,
    x_send,
    across_recv,
    pair_send,
    pair_recv,
    rp_send,
    rp_recv,
    rx_send,
    rx_recv,
    rz_send,
    rz_recv,
    rf_send,
    rf_recv,
):
    dp, tm = lax.axis_index("dp"), lax.axis_index("tm")
    z, x = dp // 2, dp % 2
    y, core = tm // 2, tm % 2
    frames, hw, width = clip_hbm.shape
    wide = cot_hbm.shape[-1]
    half = wide // 2
    rows = frames * hw
    cols = width * 3 // 4
    window = -(-cols // LANES) * LANES
    stride = cols // LANES * LANES
    scale = 1.0 / math.sqrt(width)
    span = nz - 1
    zh = nz // 2
    distances = [d for k in range(1, nz) for d in (-k, k)]

    across = (z * 2 + 1 - x, tm)
    pair = (dp, y * 2 + 1 - core)

    def along_z(d):
        return ((z + d) * 2 + x, tm)

    def there(d):
        return jnp.logical_and(z + d >= 0, z + d < nz)

    def remote(source, target, send, recv, device):
        return pltpu.make_async_remote_copy(
            src_ref=source,
            dst_ref=target,
            send_sem=send,
            recv_sem=recv,
            device_id=device,
            device_id_type=MESH,
        )

    def start_when(condition, copy):
        pl.when(condition)(lambda: copy().start())

    locals_ = [
        pltpu.make_async_copy(clip_hbm, clip, local_sem.at[0]),
        pltpu.make_async_copy(qkv_w_hbm, qkv_w, local_sem.at[1]),
        pltpu.make_async_copy(gain_hbm, gain, local_sem.at[6]),
        pltpu.make_async_copy(taps_hbm, taps.at[dp], local_sem.at[2]),
        pltpu.make_async_copy(cot_hbm, cot.at[pl.ds(0, frames)], local_sem.at[3]),
        pltpu.make_async_copy(out_w_hbm, out_w, local_sem.at[4]),
    ]
    barrier = pltpu.get_barrier_semaphore()
    for target in (across, *((dp, (tm + i) % 4) for i in range(1, 4))):
        pl.semaphore_signal(barrier, inc=1, device_id=target, device_id_type=MESH)
    for d in distances:
        pl.when(there(d))(
            lambda d=d: pl.semaphore_signal(
                barrier, inc=1, device_id=along_z(d), device_id_type=MESH
            )
        )
    for copy in locals_:
        copy.start()
    pl.semaphore_wait(barrier, 4 + span)

    my_half = pl.ds(pl.multiple_of(core * half, LANES), half)
    pair_half = pl.ds(pl.multiple_of((1 - core) * half, LANES), half)

    def part(c):
        return pl.ds(*CHUNKS[c])

    def slot(line, d, c):
        return taps.at[(z + d) * 2 + line, part(c), :, my_half]

    def held(d, c):
        return taps_hbm.at[part(c), :, my_half] if d == 0 else slot(x, d, c)

    def z_copy(d, c):
        return remote(
            held(0, c),
            slot(x, 0, c),
            z_send.at[d + span, c],
            line_recv.at[span - d, c],
            along_z(d),
        )

    def across_copy(d, c):
        return remote(
            held(d, c), slot(x, d, c), x_send.at[d + span, c], across_recv.at[d + span, c], across
        )

    def pair_copy(line, d, c):
        where = slot(1 - x if line else x, d, c)
        return remote(
            where, where, pair_send.at[line, d + span, c], pair_recv.at[line, d + span, c], pair
        )

    def line_wait(d, c):
        where = slot(x, d, c)
        remote(where, where, z_send.at[d + span, c], line_recv.at[d + span, c], pair).wait_recv()

    def across_wait(d, c):
        where = slot(1 - x, d, c)
        remote(
            where, where, x_send.at[d + span, c], across_recv.at[d + span, c], across
        ).wait_recv()

    def pair_wait(line, d, c):
        where = taps.at[(z + d) * 2 + (1 - x if line else x), part(c), :, pair_half]
        remote(
            where, where, pair_send.at[line, d + span, c], pair_recv.at[line, d + span, c], pair
        ).wait_recv()

    def cot_copy(f):
        return remote(cot_hbm.at[f], cot.at[frames + f], cot_send.at[f], cot_recv.at[f], (dp, tm - 1))

    for c in range(len(CHUNKS)):
        across_copy(0, c).start()
        for d in distances:
            start_when(there(d), lambda: z_copy(d, c))
    for f in range(frames):
        start_when(tm > 0, lambda: cot_copy(f))

    def pass_on(d, c):
        @pl.when(there(d))
        def _():
            line_wait(d, c)
            across_copy(d, c).start()
            pair_copy(0, d, c).start()

    def pass_across(d, c):
        @pl.when(there(d))
        def _():
            across_wait(d, c)
            pair_copy(1, d, c).start()

    def project():
        locals_[0].wait()
        locals_[1].wait()
        locals_[2].wait()
        features = clip[...].reshape(rows, width).astype(F32)
        squares = jnp.mean(features * features, axis=-1, keepdims=True)
        normed_bf = (features * lax.rsqrt(squares + 1e-06) * gain[...].reshape(1, width)).astype(BF16)
        normed[...] = normed_bf
        qkv[...] = matmul(normed_bf, qkv_w[...], PLAIN).astype(BF16)

    def attend(f):
        at = pl.ds(f * hw, hw)
        scores = matmul(qkv[at, 0:width], qkv[at, width : 2 * width], RIGHT_T) * scale
        weights = jnp.exp(scores - jnp.max(scores, axis=-1, keepdims=True))
        weights = weights / jnp.sum(weights, axis=-1, keepdims=True)
        probs[f] = weights
        weights_t[f] = weights.astype(BF16).T

    def turn():
        normed_t[...] = normed[...].T

    @pl.when(tm == 3)
    def _():
        cot[frames : 2 * frames] = jnp.zeros((frames, hw, wide), BF16)

    def add_taps(c):
        for d in [0] + distances:
            if d:
                pl.when(there(d))(lambda: pair_wait(0, d, c))
            pl.when(there(d))(lambda: pair_wait(1, d, c))
        if c == 0:
            locals_[3].wait()
            locals_[4].wait()
            locals_[5].wait()
        else:
            for f in range(frames):
                pl.when(tm < 3)(lambda: cot_copy(f).wait_recv())
        first, count = CHUNKS[c]
        added = None
        for tap in range(first, first + count):
            term = matmul(
                cot[2 - tap : 2 - tap + frames].reshape(rows, wide),
                taps[:, tap].reshape(width, wide),
                RIGHT_T,
            )
            added = term if added is None else added + term
        if c == 0:
            total[...] = added
        else:
            upstream[...] = (total[...] + added).astype(BF16)

    project()
    pass_on(-1, 0)
    pass_on(1, 0)
    attend(0)
    for d in distances[2:]:
        pass_on(d, 0)
    attend(1)
    pass_across(0, 0)
    for d in distances:
        pass_on(d, 1)
    turn()
    for d in distances:
        pass_across(d, 0)
    add_taps(0)
    for d in [0] + distances:
        pass_across(d, 1)
    add_taps(1)

    own_z = pl.ds(core * zh, zh)
    owner = z // zh == core

    def rp_copy(g):
        return remote(
            grad.at[g, pl.ds((1 - core) * zh, zh)], pair_in.at[g], rp_send.at[g], rp_recv.at[g], pair
        )

    def rx_copy(g):
        return remote(x_out.at[g], x_in.at[g], rx_send.at[g], rx_recv.at[g], across)

    def rz_copy(g, d):
        return remote(
            z_out.at[g, z + d - core * zh],
            z_in.at[g, span - d],
            rz_send.at[g, span + d],
            rz_recv.at[g, span - d],
            along_z(d),
        )

    def rz_wait(g, d):
        remote(
            z_in.at[g, span + d],
            z_in.at[g, span + d],
            rz_send.at[g, span + d],
            rz_recv.at[g, span + d],
            along_z(d),
        ).wait_recv()

    def to_z(d):
        return jnp.logical_and(there(d), (z + d) // zh == core)

    def reduce_local(g):
        block = qkv_cot[:, g * width : (g + 1) * width]
        grad[g] = matmul(normed_t[...], block, PLAIN).astype(BF16).reshape(nz, 2, -1, width)
        rp_copy(g).start()

    def reduce_x(g):
        rp_copy(g).wait_recv()
        x_out[g] = (
            grad[g, own_z, 1 - x].astype(F32) + pair_in[g, :, 1 - x].astype(F32)
        ).astype(BF16)
        rx_copy(g).start()
        kept[g] = grad[g, own_z, x].astype(F32) + pair_in[g, :, x].astype(F32)

    def reduce_z(g):
        rx_copy(g).wait_recv()
        sums = kept[g] + x_in[g].astype(F32)
        kept[g] = sums
        z_out[g] = sums.astype(BF16)
        for d in reversed(distances):
            start_when(to_z(d), lambda: rz_copy(g, d))

    def reduce_end(g):
        @pl.when(owner)
        def _():
            mine = z - core * zh
            for d in distances:

                @pl.when(there(d))
                def _(d=d):
                    rz_wait(g, d)
                    kept[g, mine] = kept[g, mine] + z_in[g, span + d].astype(F32)

            slab[:, g * width : (g + 1) * width] = kept[g, mine].astype(BF16)

    def columns(t):
        return pl.ds(t * stride, window)

    mixed_cot[...] = matmul(upstream[...], out_w[...], RIGHT_T).astype(BF16)
    for f in range(frames):
        at = pl.ds(f * hw, hw)
        qkv_cot[at, 2 * width : 3 * width] = matmul(weights_t[f], mixed_cot[at, :], PLAIN).astype(
            BF16
        )
    reduce_local(2)
    for f in range(frames):
        at = pl.ds(f * hw, hw)
        p = probs[f]
        d_weights = matmul(mixed_cot[at, :], qkv[at, 2 * width : 3 * width], RIGHT_T)
        d_weights = d_weights.astype(BF16).astype(F32)
        inner = jnp.sum(p * d_weights, axis=-1, keepdims=True)
        d_scores = (p * (d_weights - inner) * scale).astype(BF16)
        qkv_cot[at, 0:width] = matmul(d_scores, qkv[at, width : 2 * width], PLAIN).astype(BF16)
        qkv_cot[at, width : 2 * width] = matmul(d_scores, qkv[at, 0:width], LEFT_T).astype(BF16)
        if f == 0:
            reduce_x(2)
    reduce_local(0)
    reduce_local(1)
    reduce_z(2)
    reduce_x(0)
    reduce_x(1)

    features = clip[...].reshape(rows, width).astype(F32)
    squares = jnp.mean(features * features, axis=-1, keepdims=True)
    root = lax.rsqrt(squares + 1e-06)
    total[...] = matmul(qkv_cot[...], qkv_w[...], RIGHT_T) * gain[...].reshape(1, width)
    reduce_z(0)
    lean = jnp.mean(features * total[...], axis=-1, keepdims=True)
    direct = root * total[...] - features * (root * root * root * lean)
    grad_in[...] = (upstream[...].astype(F32) + direct).astype(BF16).reshape(frames, hw, width)
    result_copy = pltpu.make_async_copy(grad_in, grad_in_hbm, local_sem.at[5])
    result_copy.start()
    reduce_z(1)
    for f in range(frames):
        pl.when(tm > 0)(lambda: cot_copy(f).wait_send())
    for c in range(len(CHUNKS)):
        across_copy(0, c).wait_send()
        pair_copy(1, 0, c).wait_send()
        for d in distances:

            @pl.when(there(d))
            def _():
                z_copy(d, c).wait_send()
                across_copy(d, c).wait_send()
                pair_copy(0, d, c).wait_send()
                pair_copy(1, d, c).wait_send()

    for g in (2, 0, 1):
        reduce_end(g)

    def slab_copy(t):
        return remote(
            slab.at[:, columns(t)], slab_in.at[y], rf_send.at[t], rf_recv.at[y], (dp, t)
        )

    for t in range(4):
        start_when(jnp.logical_and(owner, tm != t), lambda: slab_copy(t))
    for source in range(2):
        local = jnp.logical_and(owner, y == source)

        @pl.when(local)
        def _():
            at = pl.ds(pl.multiple_of(tm * stride, LANES), window)
            slab_in[source] = slab[:, at]

        @pl.when(jnp.logical_not(local))
        def _():
            remote(
                slab_in.at[source], slab_in.at[source], rf_send.at[0], rf_recv.at[source], pair
            ).wait_recv()

    sums = slab_in[0].astype(F32) + slab_in[1].astype(F32)
    for t in range(4):

        @pl.when(tm == t)
        def _(t=t):
            first = t * (cols - stride)
            grad_w[...] = sums[:, first : first + cols]

    weight_copy = pltpu.make_async_copy(grad_w, grad_w_hbm, local_sem.at[7])
    weight_copy.start()

    for g in range(3):
        rp_copy(g).wait_send()
        rx_copy(g).wait_send()
        for d in distances:
            pl.when(to_z(d))(lambda: rz_copy(g, d).wait_send())
    for t in range(4):
        pl.when(jnp.logical_and(owner, tm != t))(lambda: slab_copy(t).wait_send())
    result_copy.wait()
    weight_copy.wait()


def on_device(
    ndp, ntm, clip_input, norm_gain, qkv_weight, out_weight, time_weight, upsample_cotangent
):
    _, frames, hw, width = clip_input.shape
    wide = upsample_cotangent.shape[-1]
    share = width // ndp
    fits = ndp % 4 == 0 and ntm == 4 and frames == 2 and share % 16 == 0
    if not fits or width % LANES or wide % (2 * LANES):
        return on_device_by_collectives(
            clip_input, norm_gain, qkv_weight, out_weight, time_weight, upsample_cotangent
        )
    nz = ndp // 2
    cols = 3 * width // ntm
    window = -(-cols // LANES) * LANES
    rows = frames * hw
    steps = 2 * nz - 1
    chunks = len(CHUNKS)
    anywhere = pl.BlockSpec(memory_space=pl.ANY)
    dma = pltpu.SemaphoreType.DMA
    grad_in, grad_w = pl.pallas_call(
        functools.partial(fused_kernel, nz),
        out_shape=(
            jax.ShapeDtypeStruct((frames, hw, width), BF16),
            jax.ShapeDtypeStruct((share, cols), F32),
        ),
        in_specs=[anywhere] * 6,
        out_specs=(anywhere, anywhere),
        scratch_shapes=[
            pltpu.VMEM((frames, hw, width), BF16),
            pltpu.VMEM((width,), F32),
            pltpu.VMEM((width, 3 * width), BF16),
            pltpu.VMEM((width, width), BF16),
            pltpu.VMEM((ndp, 3, share, wide), BF16),
            pltpu.VMEM((2 * frames, hw, wide), BF16),
            pltpu.VMEM((rows, width), BF16),
            pltpu.VMEM((width, rows), BF16),
            pltpu.VMEM((rows, 3 * width), BF16),
            pltpu.VMEM((frames, hw, hw), F32),
            pltpu.VMEM((frames, hw, hw), BF16),
            pltpu.VMEM((rows, width), F32),
            pltpu.VMEM((rows, width), BF16),
            pltpu.VMEM((rows, width), BF16),
            pltpu.VMEM((rows, 3 * width), BF16),
            pltpu.VMEM((frames, hw, width), BF16),
            pltpu.VMEM((share, cols), F32),
            pltpu.VMEM((3, nz, 2, share, width), BF16),
            pltpu.VMEM((3, nz // 2, 2, share, width), BF16),
            pltpu.VMEM((3, nz // 2, share, width), F32),
            pltpu.VMEM((3, nz // 2, share, width), BF16),
            pltpu.VMEM((3, nz // 2, share, width), BF16),
            pltpu.VMEM((3, nz // 2, share, width), BF16),
            pltpu.VMEM((3, steps, share, width), BF16),
            pltpu.VMEM((share, 3 * width), BF16),
            pltpu.VMEM((2, share, window), BF16),
            dma((8,)),
            dma((2,)),
            dma((2,)),
            dma((steps, chunks)),
            dma((steps, chunks)),
            dma((steps, chunks)),
            dma((steps, chunks)),
            dma((2, steps, chunks)),
            dma((2, steps, chunks)),
            dma((3,)),
            dma((3,)),
            dma((3,)),
            dma((3,)),
            dma((3, steps)),
            dma((3, steps)),
            dma((4,)),
            dma((2,)),
        ],
        compiler_params=pltpu.CompilerParams(
            collective_id=0, has_side_effects=True, vmem_limit_bytes=VMEM_GRANT
        ),
        cost_estimate=pl.CostEstimate(
            flops=2 * rows * width * (3 * wide + 10 * width + 6 * hw),
            bytes_accessed=4 * rows * wide + 16 * width * width,
            transcendentals=rows * hw,
        ),
    )(
        clip_input[0],
        norm_gain,
        qkv_weight,
        out_weight,
        time_weight,
        upsample_cotangent[0],
    )
    return (grad_in[None], grad_w)


def solution(mesh):
    in_specs = (
        P("dp", "tm", None, None),
        P(),
        P(),
        P(),
        P(None, "dp", None),
        P("dp", "tm", None, None),
    )
    out_specs = (P("dp", "tm", None, None), P("dp", "tm"))
    return jax.shard_map(
        functools.partial(on_device, mesh.shape["dp"], mesh.shape["tm"]),
        mesh=mesh,
        in_specs=in_specs,
        out_specs=out_specs,
        check_vma=False,
    )
```

profile of v0, /device:TPU:0, one launch (start us, length us, event | category | flops | bytes accessed | tf_op | source)
XLA Modules:
  0.0 45.9 jit_solution(11923426578242625356)
XLA Ops:
  0.6 42.8 %shard_map.77 = (bf16[2,256,384]{2,1,0:T(8,128)(2,1)}, f32[48,288]{1,0:T(8,128)}) custom-call(bf16[2,256,384]{2,1,0:T(8,128)(2,1)} %bitcast.5, f32[384]{0:T(512)} %gain_hbm.1, bf16[384,1152]{1,0:T(8,128)(2,1)} %qkv_w_hbm.1, bf16[384,384]{1,0:T(8,128)(2,1)} %out_w_hbm.1, bf16[3,48,768]{2,1,0:T(8,128)(2,1)} %taps_hbm.1, bf16[2,256,768]{2,1,0:T(8,128)(2,1)} %bitcast.4), custom_call_target="tpu_custom_call" | custom-call | flops 3019898880 | bytes 3932160 | tf_op jit(solution)/shard_map/pallas_call | solution.py:541
  43.4 0.0 copy-start
  43.4 1.8 %copy.10 = bf16[1,2,256,384]{3,2,1,0:T(8,128)(2,1)} copy(bf16[1,2,256,384]{3,2,1,0:T(8,128)(2,1)} %bitcast.3) | data formatting | bytes 786432
  45.2 0.0 copy-done
  45.2 0.6 %copy.11 = f32[48,288]{1,0:T(8,128)} copy(f32[48,288]{1,0:T(8,128)S(1)} %copy-done) | data formatting | bytes 110592
Async XLA Ops:
  43.4 1.8 %copy-start = (f32[48,288]{1,0:T(8,128)S(1)}, f32[48,288]{1,0:T(8,128)}, u32[]{:S(2)}) copy-start(f32[48,288]{1,0:T(8,128)} %get-tuple-element.9) | copy-start | bytes 165892
where the time goes:
time: 46 us; the launch traced here: 45.9 us
  Pallas kernels  42.8 us (93%)
  local copies, waits for them, and re-layouts  2.45 us (5%)
  between operations  0.65 us (1%)
    pallas_call x1, Pallas kernels, on_device(): pl.pallas_call(functools.partial(fused_kernel, nz), out_shape=(jax.ShapeD...  42.8 us
    unnamed x4, local copies, waits for them, and re-layouts  2.45 us

commit v1 on v0

--- a/solution.py
+++ b/solution.py
@@ -96,7 +96,6 @@
 PLAIN = ((1,), (0,))
 RIGHT_T = ((1,), (1,))
 LEFT_T = ((0,), (0,))
-CHUNKS = ((2, 1), (0, 2))
 
 
 def matmul(a, b, contract):
@@ -215,76 +214,62 @@
         copy.start()
     pl.semaphore_wait(barrier, 4 + span)
 
-    my_half = pl.ds(pl.multiple_of(core * half, LANES), half)
-    pair_half = pl.ds(pl.multiple_of((1 - core) * half, LANES), half)
-
-    def part(c):
-        return pl.ds(*CHUNKS[c])
-
-    def slot(line, d, c):
-        return taps.at[(z + d) * 2 + line, part(c), :, my_half]
-
-    def held(d, c):
-        return taps_hbm.at[part(c), :, my_half] if d == 0 else slot(x, d, c)
-
-    def z_copy(d, c):
+    def mine(d):
+        return jnp.logical_and(there(d), (z + d + nz) % 2 == core)
+
+    def others(d):
+        return jnp.logical_and(there(d), (z + d + nz) % 2 != core)
+
+    def slot(line, d):
+        return taps.at[(z + d) * 2 + line]
+
+    def held(d):
+        return taps_hbm if d == 0 else slot(x, d)
+
+    def z_copy(d):
+        return remote(held(0), slot(x, 0), z_send.at[d + span], line_recv.at[span - d], along_z(d))
+
+    def across_copy(d):
+        return remote(held(d), slot(x, d), x_send.at[d + span], across_recv.at[d + span], across)
+
+    def pair_copy(line, d):
+        where = slot(1 - x if line else x, d)
         return remote(
-            held(0, c),
-            slot(x, 0, c),
-            z_send.at[d + span, c],
-            line_recv.at[span - d, c],
-            along_z(d),
-        )
-
-    def across_copy(d, c):
-        return remote(
-            held(d, c), slot(x, d, c), x_send.at[d + span, c], across_recv.at[d + span, c], across
-        )
-
-    def pair_copy(line, d, c):
-        where = slot(1 - x if line else x, d, c)
-        return remote(
-            where, where, pair_send.at[line, d + span, c], pair_recv.at[line, d + span, c], pair
-        )
-
-    def line_wait(d, c):
-        where = slot(x, d, c)
-        remote(where, where, z_send.at[d + span, c], line_recv.at[d + span, c], pair).wait_recv()
-
-    def across_wait(d, c):
-        where = slot(1 - x, d, c)
-        remote(
-            where, where, x_send.at[d + span, c], across_recv.at[d + span, c], across
-        ).wait_recv()
-
-    def pair_wait(line, d, c):
-        where = taps.at[(z + d) * 2 + (1 - x if line else x), part(c), :, pair_half]
-        remote(
-            where, where, pair_send.at[line, d + span, c], pair_recv.at[line, d + span, c], pair
-        ).wait_recv()
-
-    def cot_copy(f):
-        return remote(cot_hbm.at[f], cot.at[frames + f], cot_send.at[f], cot_recv.at[f], (dp, tm - 1))
-
-    for c in range(len(CHUNKS)):
-        across_copy(0, c).start()
+            where, where, pair_send.at[line, d + span], pair_recv.at[line, d + span], pair
+        )
+
+    def line_wait(d):
+        where = slot(x, d)
+        remote(where, where, z_send.at[d + span], line_recv.at[d + span], pair).wait_recv()
+
+    def across_wait(d):
+        where = slot(1 - x, d)
+        remote(where, where, x_send.at[d + span], across_recv.at[d + span], across).wait_recv()
+
+    cot_copy = remote(
+        cot_hbm, cot.at[pl.ds(frames, frames)], cot_send.at[0], cot_recv.at[0], (dp, tm - 1)
+    )
+
+    @pl.when(mine(0))
+    def _():
+        across_copy(0).start()
         for d in distances:
-            start_when(there(d), lambda: z_copy(d, c))
-    for f in range(frames):
-        start_when(tm > 0, lambda: cot_copy(f))
-
-    def pass_on(d, c):
-        @pl.when(there(d))
+            start_when(there(d), lambda: z_copy(d))
+
+    start_when(tm > 0, lambda: cot_copy)
+
+    def pass_on(d):
+        @pl.when(mine(d))
         def _():
-            line_wait(d, c)
-            across_copy(d, c).start()
-            pair_copy(0, d, c).start()
-
-    def pass_across(d, c):
-        @pl.when(there(d))
+            line_wait(d)
+            across_copy(d).start()
+            pair_copy(0, d).start()
+
+    def pass_across(d):
+        @pl.when(mine(d))
         def _():
-            across_wait(d, c)
-            pair_copy(1, d, c).start()
+            across_wait(d)
+            pair_copy(1, d).start()
 
     def project():
         locals_[0].wait()
@@ -311,49 +296,39 @@
     def _():
         cot[frames : 2 * frames] = jnp.zeros((frames, hw, wide), BF16)
 
-    def add_taps(c):
-        for d in [0] + distances:
+    project()
+    for d in distances[:2]:
+        pass_on(d)
+    attend(0)
+    pass_across(0)
+    for d in distances[2:4]:
+        pass_on(d)
+    attend(1)
+    for d in distances[4:]:
+        pass_on(d)
+    for d in distances:
+        pass_across(d)
+    turn()
+    for d in [0] + distances:
+
+        @pl.when(others(d))
+        def _():
             if d:
-                pl.when(there(d))(lambda: pair_wait(0, d, c))
-            pl.when(there(d))(lambda: pair_wait(1, d, c))
-        if c == 0:
-            locals_[3].wait()
-            locals_[4].wait()
-            locals_[5].wait()
-        else:
-            for f in range(frames):
-                pl.when(tm < 3)(lambda: cot_copy(f).wait_recv())
-        first, count = CHUNKS[c]
-        added = None
-        for tap in range(first, first + count):
-            term = matmul(
-                cot[2 - tap : 2 - tap + frames].reshape(rows, wide),
-                taps[:, tap].reshape(width, wide),
-                RIGHT_T,
-            )
-            added = term if added is None else added + term
-        if c == 0:
-            total[...] = added
-        else:
-            upstream[...] = (total[...] + added).astype(BF16)
-
-    project()
-    pass_on(-1, 0)
-    pass_on(1, 0)
-    attend(0)
-    for d in distances[2:]:
-        pass_on(d, 0)
-    attend(1)
-    pass_across(0, 0)
-    for d in distances:
-        pass_on(d, 1)
-    turn()
-    for d in distances:
-        pass_across(d, 0)
-    add_taps(0)
-    for d in [0] + distances:
-        pass_across(d, 1)
-    add_taps(1)
+                pair_copy(0, d).wait_recv()
+            pair_copy(1, d).wait_recv()
+
+    locals_[3].wait()
+    locals_[4].wait()
+    locals_[5].wait()
+    pl.when(tm < 3)(lambda: cot_copy.wait_recv())
+    for tap in range(3):
+        term = matmul(
+            cot[2 - tap : 2 - tap + frames].reshape(rows, wide),
+            taps[:, tap].reshape(width, wide),
+            RIGHT_T,
+        )
+        added = term if tap == 0 else added + term
+    upstream[...] = added.astype(BF16)
 
     own_z = pl.ds(core * zh, zh)
     owner = z // zh == core
@@ -459,19 +434,21 @@
     result_copy = pltpu.make_async_copy(grad_in, grad_in_hbm, local_sem.at[5])
     result_copy.start()
     reduce_z(1)
-    for f in range(frames):
-        pl.when(tm > 0)(lambda: cot_copy(f).wait_send())
-    for c in range(len(CHUNKS)):
-        across_copy(0, c).wait_send()
-        pair_copy(1, 0, c).wait_send()
+    pl.when(tm > 0)(lambda: cot_copy.wait_send())
+
+    @pl.when(mine(0))
+    def _():
         for d in distances:
-
-            @pl.when(there(d))
-            def _():
-                z_copy(d, c).wait_send()
-                across_copy(d, c).wait_send()
-                pair_copy(0, d, c).wait_send()
-                pair_copy(1, d, c).wait_send()
+            pl.when(there(d))(lambda: z_copy(d).wait_send())
+
+    for d in [0] + distances:
+
+        @pl.when(mine(d))
+        def _():
+            across_copy(d).wait_send()
+            if d:
+                pair_copy(0, d).wait_send()
+            pair_copy(1, d).wait_send()
 
     for g in (2, 0, 1):
         reduce_end(g)
@@ -525,7 +502,7 @@
     _, frames, hw, width = clip_input.shape
     wide = upsample_cotangent.shape[-1]
     share = width // ndp
-    fits = ndp % 4 == 0 and ntm == 4 and frames == 2 and share % 16 == 0
+    fits = ndp % 4 == 0 and ndp >= 8 and ntm == 4 and frames == 2 and share % 16 == 0
     if not fits or width % LANES or wide % (2 * LANES):
         return on_device_by_collectives(
             clip_input, norm_gain, qkv_weight, out_weight, time_weight, upsample_cotangent
@@ -535,7 +512,6 @@
     window = -(-cols // LANES) * LANES
     rows = frames * hw
     steps = 2 * nz - 1
-    chunks = len(CHUNKS)
     anywhere = pl.BlockSpec(memory_space=pl.ANY)
     dma = pltpu.SemaphoreType.DMA
     grad_in, grad_w = pl.pallas_call(
@@ -574,14 +550,14 @@
             pltpu.VMEM((share, 3 * width), BF16),
             pltpu.VMEM((2, share, window), BF16),
             dma((8,)),
-            dma((2,)),
-            dma((2,)),
-            dma((steps, chunks)),
-            dma((steps, chunks)),
-            dma((steps, chunks)),
-            dma((steps, chunks)),
-            dma((2, steps, chunks)),
-            dma((2, steps, chunks)),
+            dma((1,)),
+            dma((1,)),
+            dma((steps,)),
+            dma((steps,)),
+            dma((steps,)),
+            dma((steps,)),
+            dma((2, steps)),
+            dma((2, steps)),
             dma((3,)),
             dma((3,)),
             dma((3,)),

time: 46 us -> 47.7 us (1.037)
  Pallas kernels: 42.8 us -> 44.5 us
    pallas_call x1, Pallas kernels: 42.8 us -> 44.5 us  [on_device(): pl.pallas_call(functools.partial(fused_kernel, nz), out_shape=(jax.ShapeD...]
where the time goes in v1:
time: 47.7 us; the launch traced here: 47.6 us
  Pallas kernels  44.5 us (93%)
  local copies, waits for them, and re-layouts  2.45 us (5%)
  between operations  0.65 us (1%)
    pallas_call x1, Pallas kernels, on_device(): pl.pallas_call(functools.partial(fused_kernel, nz), out_shape=(jax.ShapeD...  44.5 us
    unnamed x4, local copies, waits for them, and re-layouts  2.45 us

profile of v1, /device:TPU:0, one launch (start us, length us, event | category | flops | bytes accessed | tf_op | source)
XLA Modules:
  0.0 47.6 jit_solution(9721815351546558438)
XLA Ops:
  0.6 44.5 %shard_map.77 = (bf16[2,256,384]{2,1,0:T(8,128)(2,1)}, f32[48,288]{1,0:T(8,128)}) custom-call(bf16[2,256,384]{2,1,0:T(8,128)(2,1)} %bitcast.5, f32[384]{0:T(512)} %gain_hbm.1, bf16[384,1152]{1,0:T(8,128)(2,1)} %qkv_w_hbm.1, bf16[384,384]{1,0:T(8,128)(2,1)} %out_w_hbm.1, bf16[3,48,768]{2,1,0:T(8,128)(2,1)} %taps_hbm.1, bf16[2,256,768]{2,1,0:T(8,128)(2,1)} %bitcast.4), custom_call_target="tpu_custom_call" | custom-call | flops 3019898880 | bytes 3932160 | tf_op jit(solution)/shard_map/pallas_call | solution.py:517
  45.1 0.0 copy-start
  45.2 1.8 %copy.10 = bf16[1,2,256,384]{3,2,1,0:T(8,128)(2,1)} copy(bf16[1,2,256,384]{3,2,1,0:T(8,128)(2,1)} %bitcast.3) | data formatting | bytes 786432
  47.0 0.0 copy-done
  47.0 0.6 %copy.11 = f32[48,288]{1,0:T(8,128)} copy(f32[48,288]{1,0:T(8,128)S(1)} %copy-done) | data formatting | bytes 110592
Async XLA Ops:
  45.1 1.8 %copy-start = (f32[48,288]{1,0:T(8,128)S(1)}, f32[48,288]{1,0:T(8,128)}, u32[]{:S(2)}) copy-start(f32[48,288]{1,0:T(8,128)} %get-tuple-element.9) | copy-start | bytes 165892

commit v2 on v0

--- a/solution.py
+++ b/solution.py
@@ -89,7 +89,7 @@
 
 
 LANES = 128
-VMEM_GRANT = 64 * 1024 * 1024 - 64 * 1024
+VMEM_GRANT = 64 * 1024 * 1024 - 704 * 1024
 MESH = pl.DeviceIdType.MESH
 F32 = jnp.float32
 BF16 = jnp.bfloat16
@@ -111,8 +111,8 @@
     out_w_hbm,
     taps_hbm,
     cot_hbm,
-    grad_in_hbm,
-    grad_w_hbm,
+    grad_in,
+    grad_w,
     clip,
     gain,
     qkv_w,
@@ -128,8 +128,6 @@
     upstream,
     mixed_cot,
     qkv_cot,
-    grad_in,
-    grad_w,
     grad,
     pair_in,
     kept,
@@ -456,8 +454,6 @@
     lean = jnp.mean(features * total[...], axis=-1, keepdims=True)
     direct = root * total[...] - features * (root * root * root * lean)
     grad_in[...] = (upstream[...].astype(F32) + direct).astype(BF16).reshape(frames, hw, width)
-    result_copy = pltpu.make_async_copy(grad_in, grad_in_hbm, local_sem.at[5])
-    result_copy.start()
     reduce_z(1)
     for f in range(frames):
         pl.when(tm > 0)(lambda: cot_copy(f).wait_send())
@@ -505,9 +501,6 @@
             first = t * (cols - stride)
             grad_w[...] = sums[:, first : first + cols]
 
-    weight_copy = pltpu.make_async_copy(grad_w, grad_w_hbm, local_sem.at[7])
-    weight_copy.start()
-
     for g in range(3):
         rp_copy(g).wait_send()
         rx_copy(g).wait_send()
@@ -515,8 +508,6 @@
             pl.when(to_z(d))(lambda: rz_copy(g, d).wait_send())
     for t in range(4):
         pl.when(jnp.logical_and(owner, tm != t))(lambda: slab_copy(t).wait_send())
-    result_copy.wait()
-    weight_copy.wait()
 
 
 def on_device(
@@ -541,11 +532,11 @@
     grad_in, grad_w = pl.pallas_call(
         functools.partial(fused_kernel, nz),
         out_shape=(
-            jax.ShapeDtypeStruct((frames, hw, width), BF16),
-            jax.ShapeDtypeStruct((share, cols), F32),
+            pltpu.VMEM((frames, hw, width), BF16),
+            pltpu.VMEM((share, cols), F32),
         ),
         in_specs=[anywhere] * 6,
-        out_specs=(anywhere, anywhere),
+        out_specs=(pl.BlockSpec(memory_space=pltpu.VMEM),) * 2,
         scratch_shapes=[
             pltpu.VMEM((frames, hw, width), BF16),
             pltpu.VMEM((width,), F32),
@@ -562,8 +553,6 @@
             pltpu.VMEM((rows, width), BF16),
             pltpu.VMEM((rows, width), BF16),
             pltpu.VMEM((rows, 3 * width), BF16),
-            pltpu.VMEM((frames, hw, width), BF16),
-            pltpu.VMEM((share, cols), F32),
             pltpu.VMEM((3, nz, 2, share, width), BF16),
             pltpu.VMEM((3, nz // 2, 2, share, width), BF16),
             pltpu.VMEM((3, nz // 2, share, width), F32),

time: 46 us -> 44.4 us (0.965)
  local copies, waits for them, and re-layouts: 2.45 us -> 1.38 us
  Pallas kernels: 42.8 us -> 42.2 us
    unnamed x4 -> x2, local copies, waits for them, and re-layouts: 2.45 us -> 1.38 us
    pallas_call x1, Pallas kernels: 42.8 us -> 42.2 us  [on_device(): pl.pallas_call(functools.partial(fused_kernel, nz), out_shape=(pltpu.VMEM...]
where the time goes in v2:
time: 44.4 us; the launch traced here: 44.2 us
  Pallas kernels  42.2 us (95%)
  local copies, waits for them, and re-layouts  1.38 us (3%)
  between operations  0.64 us (1%)
    pallas_call x1, Pallas kernels, on_device(): pl.pallas_call(functools.partial(fused_kernel, nz), out_shape=(pltpu.VMEM...  42.2 us
    unnamed x2, local copies, waits for them, and re-layouts  1.38 us

profile of v2, /device:TPU:0, one launch (start us, length us, event | category | flops | bytes accessed | tf_op | source)
XLA Modules:
  0.0 44.2 jit_solution(3961646821313515324)
XLA Ops:
  0.6 42.2 %shard_map.77 = (bf16[2,256,384]{2,1,0:T(8,128)(2,1)S(1)}, f32[48,288]{1,0:T(8,128)S(1)}) custom-call(bf16[2,256,384]{2,1,0:T(8,128)(2,1)} %bitcast.5, f32[384]{0:T(512)} %gain_hbm.1, bf16[384,1152]{1,0:T(8,128)(2,1)} %qkv_w_hbm.1, bf16[384,384]{1,0:T(8,128)(2,1)} %out_w_hbm.1, bf16[3,48,768]{2,1,0:T(8,128)(2,1)} %taps_hbm.1, bf16[2,256,768]{2,1,0:T(8,128)(2,1)} %bitcast.4), custom_call_target="tpu_custom_call" | custom-call | flops 3019898880 | bytes 3932160 | tf_op jit(solution)/shard_map/pallas_call | solution.py:532
  42.8 0.7 %copy.10 = bf16[1,2,256,384]{3,2,1,0:T(8,128)(2,1)} copy(bf16[1,2,256,384]{3,2,1,0:T(8,128)(2,1)S(1)} %bitcast.3) | data formatting | bytes 786432
  43.6 0.6 %copy.11 = f32[48,288]{1,0:T(8,128)} copy(f32[48,288]{1,0:T(8,128)S(1)} %get-tuple-element.7) | data formatting | bytes 110592
